TPU v7x, 32 devices: a whole 2x2x4 slice. The times are simulated.
32 devices in a mesh: slab: 4 (over y, x), brick: 8 (over z, core).
Axes of the slice: x: 2, y: 2, z: 4, core: 2. Of those that a mesh axis runs over, the one named last changes fastest.
Arguments:
- occupancy: int32 [16, 64, 512], P('slab', 'brick'), may hold values 0 or 1
- modulus: float32 [16, 64, 512], P('slab', 'brick'), may hold values from 0.5 to 4
- displacement_start: float32 [2, 3, 16, 64, 512], P(None, None, 'slab', 'brick'), may hold values from -12 to 12
- direction_start: float32 [2, 3, 16, 64, 512], P(None, None, 'slab', 'brick'), may hold values from -12 to 12
- muscle_force: float32 [2, 40], replicated, may hold values from 16 to 512
- muscle_direction: float32 [2, 40, 3], replicated, may hold values from -4 to 4
- attachment_nodes: int32 [40, 128, 3], replicated, may hold values from 0 to 511, as said below
Outputs:
- displacement: float32 [2, 3, 16, 64, 512], P(None, None, 'slab', 'brick')
- sensitivity: float32 [2, 40], replicated
Inputs may be any that keep to these rules, and one draw needn't show every extreme that they name: attachment_nodes[m, k] holds an x index below 16, a y index below 64 and a z index below 512; the nodes of one muscle lie within 4 indices of a centre along each dimension, and may repeat.
All inputs are finite; a program needn't handle non-finite values. No bound on the sum of `occupancy` on one device may be relied on, other than what follows from the above.
Results may differ from a plain program's by a relative error of at most 0.00028.
Values sent between devices are 32-bit elements; how exact they have to be, the bound alone decides.
A program may use at most 64 MiB of HBM per device.

v0:
```python
import math

import jax
import jax.numpy as jnp
import numpy as np
from jax import lax
from jax.sharding import PartitionSpec as P

ITERS = 2
MUSCLES = 40
ATTACH = 128
FRAMES = 2


ersatz_modulus = 0.02


def passed_along(value, axis, steps):
    count = lax.axis_size(axis)
    leading, last = (max(0, -steps), min(count, count - steps))
    return lax.ppermute(value, axis, [(source, source + steps) for source in range(leading, last)])


def corner_offsets():
    return [(step_x, step_y, step_z) for step_x in (0, 1) for step_y in (0, 1) for step_z in (0, 1)]


def element_matrix():
    poisson = 0.3
    lame_first = poisson / ((1.0 + poisson) * (1.0 - 2.0 * poisson))
    shear_modulus = 0.5 / (1.0 + poisson)
    elastic = np.zeros((6, 6))
    elastic[:3, :3] = lame_first
    for position in range(3):
        elastic[position, position] += 2.0 * shear_modulus
        elastic[position + 3, position + 3] = shear_modulus
    points = [0.5 - 0.5 / math.sqrt(3.0), 0.5 + 0.5 / math.sqrt(3.0)]
    matrix = np.zeros((24, 24))
    for point_x in points:
        for point_y in points:
            for point_z in points:
                strain = np.zeros((6, 24))
                for corner, (step_x, step_y, step_z) in enumerate(corner_offsets()):
                    weight_x = point_x if step_x else 1.0 - point_x
                    weight_y = point_y if step_y else 1.0 - point_y
                    weight_z = point_z if step_z else 1.0 - point_z
                    sign_x = 1.0 if step_x else -1.0
                    sign_y = 1.0 if step_y else -1.0
                    sign_z = 1.0 if step_z else -1.0
                    grad_x = sign_x * weight_y * weight_z
                    grad_y = weight_x * sign_y * weight_z
                    grad_z = weight_x * weight_y * sign_z
                    column = 3 * corner
                    strain[0, column] = grad_x
                    strain[1, column + 1] = grad_y
                    strain[2, column + 2] = grad_z
                    strain[3, column] = grad_y
                    strain[3, column + 1] = grad_x
                    strain[4, column + 1] = grad_z
                    strain[4, column + 2] = grad_y
                    strain[5, column] = grad_z
                    strain[5, column + 2] = grad_x
                matrix += strain.T @ elastic @ strain / 8.0
    return matrix.astype(np.float32)


def element_forces(extended, element_scale, blocked_stiffness):
    extent_x, extent_y, extent_z = element_scale.shape
    corners = corner_offsets()
    stacked = jnp.stack(
        [
            extended[
                :,
                :,
                step_x : step_x + extent_x,
                step_y : step_y + extent_y,
                step_z : step_z + extent_z,
            ]
            for step_x, step_y, step_z in corners
        ]
    )
    forces = jnp.einsum(
        "biaj,afjxyz->bfixyz", blocked_stiffness, stacked, precision=lax.Precision.HIGHEST
    )
    forces = forces * element_scale[None, None, None]
    summed = None
    for corner, (step_x, step_y, step_z) in enumerate(corners):
        padded = jnp.pad(
            forces[corner],
            ((0, 0), (0, 0), (step_x, 1 - step_x), (step_y, 1 - step_y), (step_z, 1 - step_z)),
        )
        summed = padded if summed is None else summed + padded
    return summed


def element_diagonal(element_scale, diagonal_terms):
    summed = None
    for corner, (step_x, step_y, step_z) in enumerate(corner_offsets()):
        terms = element_scale[None, None] * diagonal_terms[corner][None, :, None, None, None]
        padded = jnp.pad(
            terms,
            ((0, 0), (0, 0), (step_x, 1 - step_x), (step_y, 1 - step_y), (step_z, 1 - step_z)),
        )
        summed = padded if summed is None else summed + padded
    return summed


def fold_back(summed):
    summed = summed[:, :, :, :, :-1]
    face_plane = summed[:, :, -1]
    received = passed_along(face_plane, "slab", 1)
    summed = summed[:, :, :-1].at[:, :, 0].add(received)
    face_column = summed[:, :, :, -1]
    received_column = passed_along(face_column, "brick", 1)
    return summed[:, :, :, :-1].at[:, :, :, 0].add(received_column)


def upper_faces(nodal_values):
    upper_plane = passed_along(nodal_values[:, :, :1], "slab", -1)
    extended = jnp.concatenate([nodal_values, upper_plane], axis=2)
    upper_side = passed_along(extended[:, :, :, :1], "brick", -1)
    extended = jnp.concatenate([extended, upper_side], axis=3)
    return jnp.pad(extended, ((0, 0), (0, 0), (0, 0), (0, 0), (0, 1)))


def per_frame(values):
    return values[:, None, None, None, None]


def frame_sums(left, right):
    return jnp.sum(left * right, axis=(1, 2, 3, 4))


def norm_total(residual, preconditioned):
    return lax.psum(frame_sums(residual, preconditioned), ("slab", "brick"))


def on_device(
    occupancy,
    modulus,
    displacement_start,
    direction_start,
    muscle_force,
    muscle_direction,
    attachment_nodes,
):
    stiffness = jnp.asarray(element_matrix(), dtype=jnp.float32)
    blocked_stiffness = stiffness.reshape(8, 3, 8, 3)
    diagonal_terms = jnp.diagonal(stiffness).reshape(8, 3)
    bone = occupancy.astype(jnp.float32)
    stiffness_scale = bone * modulus + (1.0 - bone) * ersatz_modulus
    size_x, size_y, size_z = stiffness_scale.shape

    def apply_operator(nodal_values):
        extended = upper_faces(nodal_values)
        return fold_back(element_forces(extended, stiffness_scale, blocked_stiffness))

    diagonal = fold_back(element_diagonal(stiffness_scale, diagonal_terms))
    anchor_x = lax.axis_index("slab") * size_x
    anchor_y = lax.axis_index("brick") * size_y
    local_x = attachment_nodes[:, :, 0].reshape(-1) - anchor_x
    local_y = attachment_nodes[:, :, 1].reshape(-1) - anchor_y
    local_z = attachment_nodes[:, :, 2].reshape(-1)
    grid_x = lax.iota(jnp.int32, size_x)
    grid_y = lax.iota(jnp.int32, size_y)
    grid_z = lax.iota(jnp.int32, size_z)
    hits_x = grid_x[:, None, None] == local_x[None, None, :]
    hits_y = grid_y[None, :, None] == local_y[None, None, :]
    plane_hits = (hits_x & hits_y).astype(jnp.float32).reshape(size_x * size_y, -1)
    depth_hits = (local_z[:, None] == grid_z[None, :]).astype(jnp.float32)
    muscle_loads = muscle_force[:, :, None] * muscle_direction / ATTACH
    values = jnp.broadcast_to(
        jnp.transpose(muscle_loads, (0, 2, 1))[:, :, :, None], (FRAMES, 3, MUSCLES, ATTACH)
    ).reshape(FRAMES * 3, MUSCLES * ATTACH)
    placed = (values[:, None, :] * plane_hits[None]).reshape(
        FRAMES * 3 * size_x * size_y, MUSCLES * ATTACH
    )
    load_field = jnp.dot(placed, depth_hits, precision=lax.Precision.HIGHEST).reshape(
        FRAMES, 3, size_x, size_y, size_z
    )
    displacement = displacement_start
    residual = load_field - apply_operator(displacement_start)
    preconditioned = residual / diagonal
    direction = direction_start
    weighted = norm_total(residual, preconditioned)
    for iteration in range(ITERS):
        stiff_image = apply_operator(direction)
        curvature = lax.psum(frame_sums(direction, stiff_image), ("slab", "brick"))
        step_length = weighted / curvature
        displacement = displacement + per_frame(step_length) * direction
        residual = residual - per_frame(step_length) * stiff_image
        if iteration + 1 < ITERS:
            preconditioned = residual / diagonal
            weighted_next = norm_total(residual, preconditioned)
            direction = preconditioned + per_frame(weighted_next / weighted) * direction
            weighted = weighted_next
    columns = displacement.reshape(FRAMES * 3 * size_x * size_y, size_z)
    sampled = lax.dot_general(
        columns, depth_hits, (((1,), (1,)), ((), ())), precision=lax.Precision.HIGHEST
    )
    sampled = sampled.reshape(FRAMES * 3, size_x * size_y, MUSCLES * ATTACH) * plane_hits[None]
    gathered = jnp.sum(sampled, axis=1).reshape(FRAMES, 3, MUSCLES, ATTACH)
    partial_terms = (
        jnp.einsum("fmc,fcma->fm", muscle_direction, gathered, precision=lax.Precision.HIGHEST)
        / ATTACH
    )
    sensitivity = lax.psum(partial_terms, ("slab", "brick"))
    return (displacement, sensitivity)


def solution(mesh):
    return jax.shard_map(
        on_device,
        mesh=mesh,
        in_specs=(
            P("slab", "brick", None),
            P("slab", "brick", None),
            P(None, None, "slab", "brick", None),
            P(None, None, "slab", "brick", None),
            P(),
            P(),
            P(),
        ),
        out_specs=(P(None, None, "slab", "brick", None), P()),
        check_vma=False,
    )
```

profile of v0, /device:TPU:0, one launch (start us, length us, event | category | flops | bytes accessed | tf_op | source)
XLA Modules:
  0.0 318.3 jit_solution(8326690782261349023)
XLA Ops:
  1.6 1.4 collective-permute-start.6
  3.9 1.3 collective-permute-start
  5.2 1.5 gather_fusion
  7.7 1.6 broadcast_multiply_fusion.7
  9.3 2.1 pad_add_fusion.3
  11.4 6.1 %collective-permute-start.4 = (f32[1,3,9,512]{3,0,2,1:T(1,128)S(1)}, f32[1,3,9,512]{3,0,2,1:T(1,128)S(1)}, u32[]{:S(2)}, u32[]{:S(2)}) collective-permute-start(f32[1,3,9,512]{3,0,2,1:T(1,128)S(1)} %slice_bitcast_fusion.28), channel_id=1, source_target_pairs={{0,8},{8,16},{16,24},{1,9},{9,17},{17,25},{2,10},{10,18},{18,26},{... | collective-permute-start | bytes 165896 | tf_op jit(solution)/shard_map/ppermute | solution.py:21
  19.6 1.5 collective-permute-start.5
  25.3 1.3 collective-permute-start.7
  26.6 1.8 collective-permute-start.1
  28.5 2.1 collective-permute-done.7
  31.3 1.2 copy.345
  32.5 1.2 copy.347
  34.8 1.2 copy.351
  40.0 1.2 copy.331
  41.2 1.2 copy.333
  42.4 1.2 copy.335
  43.6 1.2 copy.337
  44.9 1.2 copy.332
  46.0 1.2 copy.334
  48.3 8.0 %stack.98 = f32[8,2,3,4,8,512]{5,0,2,4,3,1:T(8,128)S(1)} concatenate(f32[1,2,3,4,8,512]{5,0,2,4,3,1:T(1,128)} %copy.344, f32[1,2,3,4,8,512]{5,0,2,4,3,1:T(1,128)} %copy.345, f32[1,2,3,4,8,512]{5,0,2,4,3,1:T(1,128)} %copy.346, f32[1,2,3,4,8,512]{5,0,2,4,3,1:T(1,128)} %copy.347, f32[1,2,3,4,8,512]{5,0,2,4,3,1:T(1,128)} %copy.348, f32[1,2,3,4,8,512]{5,0,2,4,3,1:T(1,128)} %copy.349, ...), dimensions={0} | concatenate | bytes 6291456 | tf_op jit(solution)/shard_map/stack | solution.py:70
  56.4 5.8 %fusion.29 = f32[2,4,8,512,8,3]{3,4,5,2,1,0:T(8,128)} fusion(f32[8,3,8,3,1,1,1]{2,0,3,1,6,5,4:T(8,128)} %constant.291, f32[8,2,3,4,8,512]{5,0,2,4,3,1:T(8,128)S(1)} %stack.98), kind=kOutput, calls=%fused_computation.26 | convolution fusion | flops 226492416 | bytes 6293760 | tf_op jit(solution)/shard_map/biaj,afjxyz->bfixyz/dot_general | solution.py:82
  62.2 8.2 %stack.89 = f32[8,2,3,4,8,512]{5,0,2,4,3,1:T(8,128)S(1)} concatenate(f32[1,2,3,4,8,512]{5,0,2,4,3,1:T(1,128)} %copy.330, f32[1,2,3,4,8,512]{5,0,2,4,3,1:T(1,128)} %copy.331, f32[1,2,3,4,8,512]{5,0,2,4,3,1:T(1,128)} %copy.332, f32[1,2,3,4,8,512]{5,0,2,4,3,1:T(1,128)} %copy.333, f32[1,2,3,4,8,512]{5,0,2,4,3,1:T(1,128)} %copy.334, f32[1,2,3,4,8,512]{5,0,2,4,3,1:T(1,128)} %copy.335, ...), dimensions={0} | concatenate | bytes 6291456 | tf_op jit(solution)/shard_map/stack | solution.py:70
  70.4 4.4 %fusion.26 = f32[2,4,8,512,8,3]{3,4,5,2,1,0:T(8,128)S(1)} fusion(f32[8,3,8,3,1,1,1]{2,0,3,1,6,5,4:T(8,128)} %constant.291, f32[8,2,3,4,8,512]{5,0,2,4,3,1:T(8,128)S(1)} %stack.89), kind=kOutput, calls=%fused_computation.25 | convolution fusion | flops 226492416 | bytes 6293760 | tf_op jit(solution)/shard_map/biaj,afjxyz->bfixyz/dot_general | solution.py:82
  74.8 4.1 %fusion.20 = (f32[8,2,3,4,8,512]{5,3,2,1,4,0:T(4,128)S(1)}, f32[8,2,3,4,8,512]{5,3,2,1,4,0:T(4,128)S(1)}) fusion(f32[2,4,8,512,8,3]{3,4,5,2,1,0:T(8,128)S(1)} %fusion.26, f32[4,8,512]{2,0,1:T(4,128)S(1)} %copy-done.8, f32[2,4,8,512,8,3]{3,4,5,2,1,0:T(8,128)S(1)} %copy-done), kind=kLoop, calls=%fused_computation.21 | loop fusion | flops 1572864 | bytes 12648448 | tf_op jit(solution)/shard_map/mul | solution.py:85
  78.9 1.9 slice_bitcast_fusion.17
  80.8 1.2 pad_add_fusion.2
  82.3 4.8 %collective-permute-start.2 = (f32[2,3,9,512]{3,0,2,1:T(2,128)S(1)}, f32[2,3,9,512]{3,0,2,1:T(2,128)S(1)}, u32[]{:S(2)}, u32[]{:S(2)}) collective-permute-start(f32[2,3,9,512]{3,0,2,1:T(2,128)S(1)} %bitcast.228), channel_id=1, source_target_pairs={{0,8},{8,16},{16,24},{1,9},{9,17},{17,25},{2,10},{10,18},{18,26},{... | collective-permute-start | bytes 331784 | tf_op jit(solution)/shard_map/ppermute | solution.py:21
  87.1 1.2 pad_add_fusion.1
  88.6 5.3 %collective-permute-start.8 = (f32[2,3,9,512]{3,0,2,1:T(2,128)S(1)}, f32[2,3,9,512]{3,0,2,1:T(2,128)S(1)}, u32[]{:S(2)}, u32[]{:S(2)}) collective-permute-start(f32[2,3,9,512]{3,0,2,1:T(2,128)S(1)} %bitcast.229), channel_id=1, source_target_pairs={{0,8},{8,16},{16,24},{1,9},{9,17},{17,25},{2,10},{10,18},{18,26},{... | collective-permute-start | bytes 331784 | tf_op jit(solution)/shard_map/ppermute | solution.py:21
  94.1 1.9 collective-permute-done.8
  97.2 3.7 %collective-permute-start.9 = (f32[2,3,4,512]{3,2,1,0:T(4,128)S(1)}, f32[2,3,4,512]{3,2,1,0:T(4,128)S(1)}, u32[]{:S(2)}, u32[]{:S(2)}) collective-permute-start(f32[2,3,4,512]{3,2,1,0:T(4,128)S(1)} %get-tuple-element.142), channel_id=1, source_target_pairs={{0,1},{1,2},{2,3},{3,4},{4,5},{5,6},{6,7},{8,9},{9,10},{10,11},{11... | collective-permute-start | bytes 147464 | tf_op jit(solution)/shard_map/ppermute | solution.py:21
  102.0 4.6 %collective-permute-start.3 = (f32[2,3,4,512]{3,2,1,0:T(4,128)S(1)}, f32[2,3,4,512]{3,2,1,0:T(4,128)S(1)}, u32[]{:S(2)}, u32[]{:S(2)}) collective-permute-start(f32[2,3,4,512]{3,2,1,0:T(4,128)S(1)} %slice_bitcast_fusion.31), channel_id=1, source_target_pairs={{0,1},{1,2},{2,3},{3,4},{4,5},{5,6},{6,7},{8,9},{9,10},{10,11},{11... | collective-permute-start | bytes 147464 | tf_op jit(solution)/shard_map/ppermute | solution.py:21
  107.5 5.1 %fusion.64 = (f32[2]{0:T(128)S(1)}, f32[2,3,4,8,512]{4,3,2,1,0:T(8,128)S(1)}) fusion(f32[3,4,8,512]{3,2,1,0:T(8,128)S(1)} %copy-done.5, f32[2,3,4,8,512]{4,2,1,0,3:T(4,128)S(1)} %fusion.68, s32[5120]{0:T(1024)S(1)} %copy-done.14, f32[4,8,5120]{2,1,0:T(8,128)S(1)} %copy-done.7, f32[2,3,5120]{2,1,0:T(4,128)S(1)} %copy-done.12), kind=kOutput, calls=%fused_computation.122 | convolution fusion | flops 6043795456 | bytes 1781768 | tf_op jit(solution)/shard_map/dot_general | solution.py:178
  112.6 40.9 %all-reduce.35 = (f32[2]{0:T(128)S(1)}, f32[2]{0:T(128)S(1)}) all-reduce(f32[2]{0:T(128)S(1)} %get-tuple-element.167, f32[2]{0:T(128)S(1)} %multiply_reduce_fusion.1), channel_id=1, replica_groups=mesh['slab'=4,'brick'=8] {'slab','brick'}, use_global_device_ids=true, to_apply=%region_1.2 | all-reduce | flops 4 | bytes 32 | tf_op jit(solution)/shard_map/psum | solution.py:135
  153.9 41.0 %psum.37 = f32[2]{0:T(128)S(1)} all-reduce(f32[2]{0:T(128)S(1)} %get-tuple-element.102), channel_id=1, replica_groups=mesh['slab'=4,'brick'=8] {'slab','brick'}, use_global_device_ids=true, to_apply=%region_5.6 | all-reduce | flops 2 | bytes 16 | tf_op jit(solution)/shard_map/psum | solution.py:135
  195.1 1.3 collective-permute-start.10
  196.4 5.5 %collective-permute-done.10 = f32[2,3,1,8,512]{4,3,2,1,0:T(8,128)S(1)} collective-permute-done((f32[2,3,1,8,512]{4,3,2,1,0:T(8,128)S(1)}, f32[2,3,1,8,512]{4,3,2,1,0:T(8,128)S(1)}, u32[]{:S(2)}, u32[]{:S(2)}) %collective-permute-start.10) | collective-permute-done | bytes 98336 | tf_op jit(solution)/shard_map/ppermute | solution.py:21
  201.9 1.5 collective-permute-start.11
  203.5 1.6 collective-permute-done.11
  206.1 5.0 %fusion.23 = f32[2,4,8,512,8,3]{3,4,5,2,1,0:T(8,128)S(1)} fusion(f32[8,3,8,3,1,1,1]{2,0,3,1,6,5,4:T(8,128)S(1)} %copy-done.11, f32[8,2,3,4,8,512,1]{5,4,3,2,1,0,6:T(8,128)S(1)} %bitcast.223), kind=kOutput, calls=%fused_computation.24 | convolution fusion | flops 226492416 | bytes 6293760 | tf_op jit(solution)/shard_map/biaj,afjxyz->bfixyz/dot_general | solution.py:82
  211.2 2.1 fusion.18
  213.9 1.2 pad_add_fusion
  215.3 4.8 %collective-permute-start.12 = (f32[2,3,9,512]{3,0,2,1:T(2,128)S(1)}, f32[2,3,9,512]{3,0,2,1:T(2,128)S(1)}, u32[]{:S(2)}, u32[]{:S(2)}) collective-permute-start(f32[2,3,9,512]{3,0,2,1:T(2,128)S(1)} %bitcast.230), channel_id=1, source_target_pairs={{0,8},{8,16},{16,24},{1,9},{9,17},{17,25},{2,10},{10,18},{18,26},{... | collective-permute-start | bytes 331784 | tf_op jit(solution)/shard_map/ppermute | solution.py:21
  220.2 2.6 collective-permute-done.12
  224.0 2.7 collective-permute-start.13
  228.0 42.3 %psum.38 = f32[2]{0:T(128)S(1)} all-reduce(f32[2]{0:T(128)S(1)} %fusion.63), channel_id=1, replica_groups=mesh['slab'=4,'brick'=8] {'slab','brick'}, use_global_device_ids=true, to_apply=%region_7.8 | all-reduce | flops 2 | bytes 16 | tf_op jit(solution)/shard_map/psum | solution.py:188
  270.5 6.9 %fusion.32 = f32[6,5120]{1,0:T(8,128)S(1)} fusion(f32[32,5120]{1,0:T(8,128)S(1)} %copy-done.6, f32[6,32,512]{2,1,0:T(8,128)S(1)} %bitcast.226, s32[5120]{0:T(1024)S(1)} %copy-done.14), kind=kOutput, calls=%fused_computation.33 | convolution fusion | flops 6044354560 | bytes 1191936 | tf_op jit(solution)/shard_map/dot_general | solution.py:198
  277.6 40.2 %psum.39 = f32[2,40]{1,0:T(2,128)} all-reduce(f32[2,40]{1,0:T(2,128)S(1)} %broadcast_multiply_fusion.8), channel_id=1, replica_groups=mesh['slab'=4,'brick'=8] {'slab','brick'}, use_global_device_ids=true, to_apply=%region_10.11 | all-reduce | flops 80 | bytes 640 | tf_op jit(solution)/shard_map/psum | solution.py:207
  (133 shorter events, 25.3 us)
Async XLA Ops:
  0.6 16.9 %copy-start.13 = (s32[40,128,3]{1,0,2:T(8,128)S(1)}, s32[40,128,3]{1,0,2:T(8,128)}, u32[]{:S(2)}) copy-start(s32[40,128,3]{1,0,2:T(8,128)} %param.30) | copy-start | bytes 184324
  1.6 17.8 %copy-start.15 = (f32[2,40,3]{1,0,2:T(2,128)S(1)}, f32[2,40,3]{1,0,2:T(2,128)}, u32[]{:S(2)}) copy-start(f32[2,40,3]{1,0,2:T(2,128)} %param.29) | copy-start | bytes 2884
  1.6 17.8 %copy-start.16 = (f32[2,40]{1,0:T(2,128)S(1)}, f32[2,40]{1,0:T(2,128)}, u32[]{:S(2)}) copy-start(f32[2,40]{1,0:T(2,128)} %param.28) | copy-start | bytes 964
  1.6 17.8 %copy-start.1 = (f32[2,3,4,8,512]{4,3,2,1,0:T(8,128)S(1)}, f32[2,3,4,8,512]{4,3,2,1,0:T(8,128)}, u32[]{:S(2)}) copy-start(f32[2,3,4,8,512]{4,3,2,1,0:T(8,128)} %param.27) | copy-start | bytes 1179652
  1.6 23.6 %collective-permute-start.6 = (f32[2,3,1,8,512]{4,3,2,1,0:T(8,128)S(1)}, f32[2,3,1,8,512]{4,3,2,1,0:T(8,128)S(1)}, u32[]{:S(2)}, u32[]{:S(2)}) collective-permute-start(f32[2,3,1,8,512]{4,3,2,1,0:T(8,128)S(1)} %slice.579), channel_id=1, source_target_pairs={{8,0},{16,8},{24,16},{9,1},{17,9},{25,17},{10,2},{18,10},{26,18},{... | collective-permute-start | bytes 294920 | tf_op jit(solution)/shard_map/ppermute | solution.py:21
  3.9 22.6 %collective-permute-start = (f32[2,3,1,8,512]{4,3,2,1,0:T(8,128)S(1)}, f32[2,3,1,8,512]{4,3,2,1,0:T(8,128)S(1)}, u32[]{:S(2)}, u32[]{:S(2)}) collective-permute-start(f32[2,3,1,8,512]{4,3,2,1,0:T(8,128)S(1)} %slice.542), channel_id=1, source_target_pairs={{8,0},{16,8},{24,16},{9,1},{17,9},{25,17},{10,2},{18,10},{26,18},{... | collective-permute-start | bytes 294920 | tf_op jit(solution)/shard_map/ppermute | solution.py:21
  7.7 13.3 %copy-start.2 = (f32[2,3,4,8,512]{4,3,2,1,0:T(8,128)S(1)}, f32[2,3,4,8,512]{4,3,2,1,0:T(8,128)}, u32[]{:S(2)}) copy-start(f32[2,3,4,8,512]{4,3,2,1,0:T(8,128)} %param.26) | copy-start | bytes 1179652
  11.4 8.0 %collective-permute-start.4 = (f32[1,3,9,512]{3,0,2,1:T(1,128)S(1)}, f32[1,3,9,512]{3,0,2,1:T(1,128)S(1)}, u32[]{:S(2)}, u32[]{:S(2)}) collective-permute-start(f32[1,3,9,512]{3,0,2,1:T(1,128)S(1)} %slice_bitcast_fusion.28), channel_id=1, source_target_pairs={{0,8},{8,16},{16,24},{1,9},{9,17},{17,25},{2,10},{10,18},{18,26},{... | collective-permute-start | bytes 165896 | tf_op jit(solution)/shard_map/ppermute | solution.py:21
  19.6 5.4 %collective-permute-start.5 = (f32[1,3,4,512]{3,0,2,1:T(1,128)S(1)}, f32[1,3,4,512]{3,0,2,1:T(1,128)S(1)}, u32[]{:S(2)}, u32[]{:S(2)}) collective-permute-start(f32[1,3,4,512]{3,0,2,1:T(1,128)S(1)} %slice_bitcast_fusion.32), channel_id=1, source_target_pairs={{0,1},{1,2},{2,3},{3,4},{4,5},{5,6},{6,7},{8,9},{9,10},{10,11},{11... | collective-permute-start | bytes 73736 | tf_op jit(solution)/shard_map/ppermute | solution.py:21
  25.2 3.3 %copy-start.4 = (f32[3,4,8,512]{3,2,1,0:T(8,128)}, f32[3,4,8,512]{3,2,1,0:T(8,128)S(1)}, u32[]{:S(2)}) copy-start(f32[3,4,8,512]{3,2,1,0:T(8,128)S(1)} %scatter-add.31) | copy-start | bytes 589828
  25.3 5.3 %collective-permute-start.7 = (f32[2,3,5,1,512]{4,3,2,1,0:T(1,128)S(1)}, f32[2,3,5,1,512]{4,3,2,1,0:T(1,128)S(1)}, u32[]{:S(2)}, u32[]{:S(2)}) collective-permute-start(f32[2,3,5,1,512]{4,3,2,1,0:T(1,128)S(1)} %slice.653), channel_id=1, source_target_pairs={{1,0},{2,1},{3,2},{4,3},{5,4},{6,5},{7,6},{9,8},{10,9},{11,10},{12... | collective-permute-start | bytes 184328 | tf_op jit(solution)/shard_map/ppermute | solution.py:21
  26.6 12.8 %collective-permute-start.1 = (f32[2,3,5,1,512]{4,3,2,1,0:T(1,128)S(1)}, f32[2,3,5,1,512]{4,3,2,1,0:T(1,128)S(1)}, u32[]{:S(2)}, u32[]{:S(2)}) collective-permute-start(f32[2,3,5,1,512]{4,3,2,1,0:T(1,128)S(1)} %slice.627), channel_id=1, source_target_pairs={{1,0},{2,1},{3,2},{4,3},{5,4},{6,5},{7,6},{9,8},{10,9},{11,10},{12... | collective-permute-start | bytes 184328 | tf_op jit(solution)/shard_map/ppermute | solution.py:21
  70.4 4.4 %copy-start = (f32[2,4,8,512,8,3]{3,4,5,2,1,0:T(8,128)S(1)}, f32[2,4,8,512,8,3]{3,4,5,2,1,0:T(8,128)}, u32[]{:S(2)}) copy-start(f32[2,4,8,512,8,3]{3,4,5,2,1,0:T(8,128)} %fusion.29) | copy-start | bytes 9437188
  70.4 4.4 %copy-start.8 = (f32[4,8,512]{2,0,1:T(4,128)S(1)}, f32[4,8,512]{2,0,1:T(4,128)}, u32[]{:S(2)}) copy-start(f32[4,8,512]{2,0,1:T(4,128)} %copy.338) | copy-start | bytes 196612
  82.3 11.7 %collective-permute-start.2 = (f32[2,3,9,512]{3,0,2,1:T(2,128)S(1)}, f32[2,3,9,512]{3,0,2,1:T(2,128)S(1)}, u32[]{:S(2)}, u32[]{:S(2)}) collective-permute-start(f32[2,3,9,512]{3,0,2,1:T(2,128)S(1)} %bitcast.228), channel_id=1, source_target_pairs={{0,8},{8,16},{16,24},{1,9},{9,17},{17,25},{2,10},{10,18},{18,26},{... | collective-permute-start | bytes 331784 | tf_op jit(solution)/shard_map/ppermute | solution.py:21
  88.3 19.2 %copy-start.5 = (f32[3,4,8,512]{3,2,1,0:T(8,128)S(1)}, f32[3,4,8,512]{3,2,1,0:T(8,128)}, u32[]{:S(2)}) copy-start(f32[3,4,8,512]{3,2,1,0:T(8,128)} %copy-done.4) | copy-start | bytes 589828
  88.3 19.2 %copy-start.7 = (f32[4,8,5120]{2,1,0:T(8,128)S(1)}, f32[4,8,5120]{2,1,0:T(8,128)}, u32[]{:S(2)}) copy-start(f32[4,8,5120]{2,1,0:T(8,128)} %get-tuple-element.155) | copy-start | bytes 1966084
  88.3 19.2 %copy-start.12 = (f32[2,3,5120]{2,1,0:T(4,128)S(1)}, f32[2,3,5120]{2,1,0:T(4,128)}, u32[]{:S(2)}) copy-start(f32[2,3,5120]{2,1,0:T(4,128)} %copy.329) | copy-start | bytes 368644
  88.3 19.2 %copy-start.14 = (s32[5120]{0:T(1024)S(1)}, s32[5120]{0:T(1024)}, u32[]{:S(2)}) copy-start(s32[5120]{0:T(1024)} %get-tuple-element.157) | copy-start | bytes 61444
  88.6 7.4 %collective-permute-start.8 = (f32[2,3,9,512]{3,0,2,1:T(2,128)S(1)}, f32[2,3,9,512]{3,0,2,1:T(2,128)S(1)}, u32[]{:S(2)}, u32[]{:S(2)}) collective-permute-start(f32[2,3,9,512]{3,0,2,1:T(2,128)S(1)} %bitcast.229), channel_id=1, source_target_pairs={{0,8},{8,16},{16,24},{1,9},{9,17},{17,25},{2,10},{10,18},{18,26},{... | collective-permute-start | bytes 331784 | tf_op jit(solution)/shard_map/ppermute | solution.py:21
  97.2 9.6 %collective-permute-start.9 = (f32[2,3,4,512]{3,2,1,0:T(4,128)S(1)}, f32[2,3,4,512]{3,2,1,0:T(4,128)S(1)}, u32[]{:S(2)}, u32[]{:S(2)}) collective-permute-start(f32[2,3,4,512]{3,2,1,0:T(4,128)S(1)} %get-tuple-element.142), channel_id=1, source_target_pairs={{0,1},{1,2},{2,3},{3,4},{4,5},{5,6},{6,7},{8,9},{9,10},{10,11},{11... | collective-permute-start | bytes 147464 | tf_op jit(solution)/shard_map/ppermute | solution.py:21
  102.0 5.5 %collective-permute-start.3 = (f32[2,3,4,512]{3,2,1,0:T(4,128)S(1)}, f32[2,3,4,512]{3,2,1,0:T(4,128)S(1)}, u32[]{:S(2)}, u32[]{:S(2)}) collective-permute-start(f32[2,3,4,512]{3,2,1,0:T(4,128)S(1)} %slice_bitcast_fusion.31), channel_id=1, source_target_pairs={{0,1},{1,2},{2,3},{3,4},{4,5},{5,6},{6,7},{8,9},{9,10},{10,11},{11... | collective-permute-start | bytes 147464 | tf_op jit(solution)/shard_map/ppermute | solution.py:21
  195.1 6.8 %collective-permute-start.10 = (f32[2,3,1,8,512]{4,3,2,1,0:T(8,128)S(1)}, f32[2,3,1,8,512]{4,3,2,1,0:T(8,128)S(1)}, u32[]{:S(2)}, u32[]{:S(2)}) collective-permute-start(f32[2,3,1,8,512]{4,3,2,1,0:T(8,128)S(1)} %slice.673), channel_id=1, source_target_pairs={{8,0},{16,8},{24,16},{9,1},{17,9},{25,17},{10,2},{18,10},{26,18},{... | collective-permute-start | bytes 294920 | tf_op jit(solution)/shard_map/ppermute | solution.py:21
  201.9 3.1 collective-permute-start.11
  205.3 0.8 copy-start.11
  206.1 5.0 %copy-start.9 = (f32[4,8,512]{2,0,1:T(4,128)S(1)}, f32[4,8,512]{2,0,1:T(4,128)}, u32[]{:S(2)}) copy-start(f32[4,8,512]{2,0,1:T(4,128)} %copy.338) | copy-start | bytes 196612
  213.9 56.4 %copy-start.3 = (f32[2,3,4,8,512]{4,3,2,1,0:T(8,128)S(1)}, f32[2,3,4,8,512]{4,3,2,1,0:T(8,128)}, u32[]{:S(2)}) copy-start(f32[2,3,4,8,512]{4,3,2,1,0:T(8,128)} %param.26) | copy-start | bytes 1179652
  215.1 55.4 %copy-start.6 = (f32[32,5120]{1,0:T(8,128)S(1)}, f32[32,5120]{1,0:T(8,128)}, u32[]{:S(2)}) copy-start(f32[32,5120]{1,0:T(8,128)} %get-tuple-element.154) | copy-start | bytes 1966084
  215.3 7.5 %collective-permute-start.12 = (f32[2,3,9,512]{3,0,2,1:T(2,128)S(1)}, f32[2,3,9,512]{3,0,2,1:T(2,128)S(1)}, u32[]{:S(2)}, u32[]{:S(2)}) collective-permute-start(f32[2,3,9,512]{3,0,2,1:T(2,128)S(1)} %bitcast.230), channel_id=1, source_target_pairs={{0,8},{8,16},{16,24},{1,9},{9,17},{17,25},{2,10},{10,18},{18,26},{... | collective-permute-start | bytes 331784 | tf_op jit(solution)/shard_map/ppermute | solution.py:21
  224.0 3.6 %collective-permute-start.13 = (f32[2,3,4,512]{3,2,1,0:T(4,128)S(1)}, f32[2,3,4,512]{3,2,1,0:T(4,128)S(1)}, u32[]{:S(2)}, u32[]{:S(2)}) collective-permute-start(f32[2,3,4,512]{3,2,1,0:T(4,128)S(1)} %slice_bitcast_fusion.29), channel_id=1, source_target_pairs={{0,1},{1,2},{2,3},{3,4},{4,5},{5,6},{6,7},{8,9},{9,10},{10,11},{11... | collective-permute-start | bytes 147464 | tf_op jit(solution)/shard_map/ppermute | solution.py:21
  270.5 7.0 %copy-start.10 = (f32[2,3,4,8,512]{4,3,2,1,0:T(8,128)}, f32[2,3,4,8,512]{4,3,2,1,0:T(8,128)S(1)}, u32[]{:S(2)}) copy-start(f32[2,3,4,8,512]{4,3,2,1,0:T(8,128)S(1)} %multiply_add_fusion) | copy-start | bytes 1179652
where the time goes:
time: 325 us; the launch traced here: 318 us
  blocking collectives  164 us (50%)
  local copies, waits for them, and re-layouts  49 us (15%)
  starting transfers between devices  42.2 us (13%)
  matrix products  27.2 us (8%)
  other arithmetic  18.8 us (6%)
  waiting for transfers between devices  14.7 us (5%)
    psum x2, blocking collectives, norm_total(): return lax.psum(frame_sums(residual, preconditioned), ('slab', 'brick'))  82 us
    psum x1, blocking collectives, on_device(): curvature = lax.psum(frame_sums(direction, stiff_image), ('slab', 'brick'))  42.3 us
    ppermute x14, starting transfers between devices, passed_along(): lax.ppermute(value, axis, [(source, source + steps) for source in range(l...  42.2 us
    psum x1, blocking collectives, on_device(): sensitivity = lax.psum(partial_terms, ('slab', 'brick'))  40.2 us
    another operation x21, local copies, waits for them, and re-layouts, element_forces(): jnp.stack([extended[:, :, step_x:step_x + extent_x, step_y:step_y + exten...  35.9 us
    dot_general x3, matrix products, element_forces(): jnp.einsum('biaj,afjxyz->bfixyz', blocked_stiffness, stacked, precision=l...  15.2 us
    ppermute x14, waiting for transfers between devices, passed_along(): lax.ppermute(value, axis, [(source, source + steps) for source in range(l...  14.7 us
    dot_general x1, matrix products, on_device(): lax.dot_general(columns, depth_hits, (((1,), (1,)), ((), ())), precision=...  6.95 us
  transfers between devices with their start and end apart: 14, of which 7 were waited for; matrix products, arithmetic and copies ran while one was open for 8% of the time, Pallas kernels for 0%

commit v1 on v0

v1 whole, which is shorter than its diff:
```python
import functools
import math

import jax
import jax.numpy as jnp
import numpy as np
from jax import lax
from jax.experimental import pallas as pl
from jax.experimental.pallas import tpu as pltpu
from jax.sharding import PartitionSpec as P

MUSCLES = 40
ATTACH = 128
FRAMES = 2
LANES = 128

ersatz_modulus = 0.02
MESH = pl.DeviceIdType.MESH
HIGHEST = lax.Precision.HIGHEST
DIRECTIONS = [(dx, dy) for dx in (-1, 0, 1) for dy in (-1, 0, 1) if (dx, dy) != (0, 0)]
LOWER = [(-1, 0), (0, -1), (-1, -1)]


def corner_offsets():
    return [(step_x, step_y, step_z) for step_x in (0, 1) for step_y in (0, 1) for step_z in (0, 1)]


def element_matrix():
    poisson = 0.3
    lame_first = poisson / ((1.0 + poisson) * (1.0 - 2.0 * poisson))
    shear_modulus = 0.5 / (1.0 + poisson)
    elastic = np.zeros((6, 6))
    elastic[:3, :3] = lame_first
    for position in range(3):
        elastic[position, position] += 2.0 * shear_modulus
        elastic[position + 3, position + 3] = shear_modulus
    points = [0.5 - 0.5 / math.sqrt(3.0), 0.5 + 0.5 / math.sqrt(3.0)]
    matrix = np.zeros((24, 24))
    for point_x in points:
        for point_y in points:
            for point_z in points:
                strain = np.zeros((6, 24))
                for corner, (step_x, step_y, step_z) in enumerate(corner_offsets()):
                    weight_x = point_x if step_x else 1.0 - point_x
                    weight_y = point_y if step_y else 1.0 - point_y
                    weight_z = point_z if step_z else 1.0 - point_z
                    sign_x = 1.0 if step_x else -1.0
                    sign_y = 1.0 if step_y else -1.0
                    sign_z = 1.0 if step_z else -1.0
                    grad_x = sign_x * weight_y * weight_z
                    grad_y = weight_x * sign_y * weight_z
                    grad_z = weight_x * weight_y * sign_z
                    column = 3 * corner
                    strain[0, column] = grad_x
                    strain[1, column + 1] = grad_y
                    strain[2, column + 2] = grad_z
                    strain[3, column] = grad_y
                    strain[3, column + 1] = grad_x
                    strain[4, column + 1] = grad_z
                    strain[4, column + 2] = grad_y
                    strain[5, column] = grad_z
                    strain[5, column + 2] = grad_x
                matrix += strain.T @ elastic @ strain / 8.0
    return matrix


def mode_terms():
    corners = corner_offsets()
    signs = np.array(
        [
            [np.prod([1.0 if (not m or s) else -1.0 for m, s in zip(mode, step)]) for step in corners]
            for mode in corners
        ]
    )
    matrix = element_matrix().reshape(8, 3, 8, 3)
    modal = np.einsum("ma,aibj,nb->minj", signs, matrix, signs) / 64.0
    terms = {}
    for m, mode in enumerate(corners):
        for i in range(3):
            row = [
                ((j,) + corners[n], float(modal[m, i, n, j]))
                for n in range(8)
                for j in range(3)
                if abs(modal[m, i, n, j]) > 1e-9
            ]
            if row:
                terms[(i,) + mode] = row
    return terms


TERMS = mode_terms()
DIAGONAL = float(element_matrix()[0, 0])


def apply_modes(modes):
    forces = {}
    for key, row in TERMS.items():
        total = None
        for other, value in row:
            term = modes[other] * value
            total = term if total is None else total + term
        forces[key] = total
    return forces


def split_rows(values):
    high = values.astype(jnp.bfloat16)
    low = (values - high.astype(jnp.float32)).astype(jnp.bfloat16)
    return jnp.concatenate([high, low], axis=0)


def kernel(
    slabs,
    bricks,
    occ_ref,
    mod_ref,
    start_ref,
    dir_ref,
    force_ref,
    line_ref,
    att_ref,
    out_ref,
    sens_ref,
    ext,
    image,
    carry_x,
    pair,
    load,
    counts,
    slab_part,
    brick_part,
    halo_send,
    halo_recv,
    pair_send,
    pair_recv,
    slab_send,
    slab_recv,
    brick_send,
    brick_recv,
):
    size_x, size_y, size_z = occ_ref.shape
    tiles = size_z // LANES
    rows = FRAMES * tiles
    slab = lax.axis_index("slab")
    brick = lax.axis_index("brick")
    barrier = pltpu.get_barrier_semaphore()

    def present(dx, dy):
        ok = None
        for delta, place, count in ((dx, slab, slabs), (dy, brick, bricks)):
            if delta == 0:
                continue
            here = (place > 0) if delta < 0 else (place < count - 1)
            ok = here if ok is None else ok & here
        return ok

    for step in range(1, slabs):
        pl.semaphore_signal(
            barrier, inc=1, device_id=(lax.rem(slab + step, slabs), brick), device_id_type=MESH
        )
    for step in range(1, bricks):
        pl.semaphore_signal(
            barrier, inc=1, device_id=(slab, lax.rem(brick + step, bricks)), device_id_type=MESH
        )
    for dx, dy in DIRECTIONS:
        if dx and dy:

            @pl.when(present(dx, dy))
            def _():
                pl.semaphore_signal(
                    barrier, inc=1, device_id=(slab + dx, brick + dy), device_id_type=MESH
                )

    flat = ext.reshape(7 * (size_x + 2) * (size_y + 2) * rows, LANES)
    zero = jnp.zeros((rows, LANES), jnp.float32)

    def place(field, x, row, value):
        base = ((field * (size_x + 2) + x + 1) * (size_y + 2) + 1) * rows + row
        flat[pl.ds(base, size_y, stride=rows), :] = value

    for x in range(size_x):
        for tile in range(tiles):
            part = slice(tile * LANES, (tile + 1) * LANES)
            bone = occ_ref[x, :, part].astype(jnp.float32)
            scale = bone * mod_ref[x, :, part] + (1.0 - bone) * ersatz_modulus
            for frame in range(FRAMES):
                row = frame * tiles + tile
                place(6, x, row, scale)
                for c in range(3):
                    place(c, x, row, start_ref[frame, c, x, :, part])
                    place(3 + c, x, row, dir_ref[frame, c, x, :, part])

    def edge(delta, size):
        if delta == 0:
            return pl.ds(1, size), pl.ds(1, size)
        return (pl.ds(1, 1), pl.ds(size + 1, 1)) if delta < 0 else (pl.ds(size, 1), pl.ds(0, 1))

    def halo(number):
        dx, dy = DIRECTIONS[number]
        source_x, target_x = edge(dx, size_x)
        source_y, target_y = edge(dy, size_y)
        fields = pl.ds(0, 7 if dx >= 0 and dy >= 0 else 6)
        return pltpu.make_async_remote_copy(
            src_ref=ext.at[fields, source_x, source_y],
            dst_ref=ext.at[fields, target_x, target_y],
            send_sem=halo_send.at[number],
            recv_sem=halo_recv.at[number],
            device_id=(slab + dx, brick + dy),
            device_id_type=MESH,
        )

    for number, (dx, dy) in enumerate(DIRECTIONS):
        back_x, back_y = edge(dx, size_x)[1], edge(dy, size_y)[1]

        @pl.when(jnp.logical_not(present(-dx, -dy)))
        def _():
            shape = (7, back_x.size, back_y.size, rows, LANES)
            ext[:, back_x, back_y] = jnp.zeros(shape, jnp.float32)

    amount = slabs + bricks - 2
    for dx, dy in DIRECTIONS:
        if dx and dy:
            amount = amount + present(dx, dy).astype(jnp.int32)
    pl.semaphore_wait(barrier, amount)

    for number, (dx, dy) in enumerate(DIRECTIONS):

        @pl.when(present(dx, dy))
        def _():
            halo(number).start()

    width = 2 * ATTACH
    span = MUSCLES * tiles
    row_ids = lax.broadcasted_iota(jnp.int32, (size_x * size_y * 2 * tiles, width), 0)
    lane_ids = lax.broadcasted_iota(jnp.int32, (LANES, width), 0)
    second = (lax.broadcasted_iota(jnp.int32, (1, width), 1) >= ATTACH).astype(jnp.int32)

    @pl.loop(0, MUSCLES // 2)
    def _(two):
        def both(dim):
            return jnp.concatenate(
                [att_ref[dim, pl.ds(2 * two, 1), :], att_ref[dim, pl.ds(2 * two + 1, 1), :]], axis=1
            )

        near_x = both(0) - slab * size_x
        near_y = both(1) - brick * size_y
        far = both(2)
        tile = lax.shift_right_logical(far, 7)
        inside = (near_x >= 0) & (near_x < size_x) & (near_y >= 0) & (near_y < size_y)
        code = ((near_x * size_y + near_y) * 2 + second) * tiles + tile
        code = jnp.where(inside, code, -1)
        hits = jnp.where(row_ids == code, 1.0, 0.0).astype(jnp.bfloat16)
        depth = jnp.where(lane_ids == far - tile * LANES, 1.0, 0.0).astype(jnp.bfloat16)
        found = lax.dot_general(
            hits, depth, (((1,), (1,)), ((), ())), preferred_element_type=jnp.float32
        )
        counts[:, pl.ds(pl.multiple_of(two * 2 * tiles, 8), 2 * tiles), :] = found.reshape(
            size_x * size_y, 2 * tiles, LANES
        )

    def iota(shape, dim):
        return lax.broadcasted_iota(jnp.int32, shape, dim)

    def dot32(left, right):
        return jnp.dot(left, right, precision=HIGHEST, preferred_element_type=jnp.float32)

    def ones_where(mask):
        return jnp.where(mask, 1.0, 0.0)

    spread_rows = ones_where(iota((24, 6), 0) // tiles == iota((24, 6), 1))
    spread_cols = ones_where(iota((MUSCLES, span), 1) // tiles == iota((MUSCLES, span), 0))
    same_tile = ones_where(iota((24, span), 0) % tiles == iota((24, span), 1) % tiles)
    lines = line_ref[...] * (1.0 / ATTACH)
    forces = jnp.concatenate([force_ref[...]] * 3, axis=0)
    line_wide = dot32(spread_rows, dot32(lines, spread_cols)) * same_tile
    load_wide = split_rows(dot32(spread_rows, dot32(lines * forces, spread_cols)) * same_tile)

    @pl.loop(0, size_x * size_y)
    def _(column):
        both = jnp.dot(
            load_wide, counts[column].astype(jnp.bfloat16), preferred_element_type=jnp.float32
        )
        load[column] = both[:24] + both[24:]

    def sampled(ref, offset):
        def body(column, total):
            x, y = column // size_y, column % size_y
            values = ref[pl.ds(0, 6), x + offset, y + offset].reshape(6 * rows, LANES)
            return total + lax.dot_general(
                split_rows(values),
                counts[column].astype(jnp.bfloat16),
                (((1,), (1,)), ((), ())),
                preferred_element_type=jnp.float32,
            )

        both = lax.fori_loop(
            0, size_x * size_y, body, jnp.zeros((12 * rows, span), jnp.float32)
        )
        total = (both[: 6 * rows] + both[6 * rows :]) * jnp.concatenate([line_wide] * 2, axis=0)
        shape = (4, 6 * rows)
        at = iota(shape, 1)
        pick = (at // 24 == iota(shape, 0) // 2) & ((at // tiles) % 2 == iota(shape, 0) % 2)
        narrow = ones_where(iota((span, LANES), 0) // tiles == iota((span, LANES), 1))
        return dot32(dot32(ones_where(pick), total), narrow)

    first_sums = sampled(ext, 1)

    lane = iota((rows, LANES), 1)
    tile_of = iota((rows, LANES), 0) % tiles
    is_last, is_first = lane == LANES - 1, lane == 0
    keep_up = ones_where(tile_of != tiles - 1)
    keep_down = ones_where(tile_of != 0)

    def from_above(value):
        turned = pltpu.roll(value, LANES - 1, 1)
        return jnp.where(is_last, pltpu.roll(turned, rows - 1, 0) * keep_up, turned)

    def from_below(value):
        turned = pltpu.roll(value, 1, 1)
        return jnp.where(is_first, pltpu.roll(turned, 1, 0) * keep_down, turned)

    def column_modes(ref, field, x, y):
        found = []
        for c in range(3):
            low, high = ref[field + c, x, y], ref[field + c, x + 1, y]
            for value in (high + low, high - low):
                above = from_above(value)
                found += [above + value, above - value]
        return tuple(found)

    def element_modes(before, after):
        modes = {}
        for c in range(3):
            for mx in (0, 1):
                for mz in (0, 1):
                    low, high = before[c * 4 + mx * 2 + mz], after[c * 4 + mx * 2 + mz]
                    modes[c, mx, 0, mz] = high + low
                    modes[c, mx, 1, mz] = high - low
        return modes

    for number, (dx, dy) in enumerate(DIRECTIONS):

        @pl.when(present(-dx, -dy))
        def _():
            halo(number).wait_recv()

    carry_x[...] = jnp.zeros_like(carry_x)

    @pl.loop(0, size_x + 1)
    def _(x):
        for half in (0, 1):

            def body(y, carry):
                before, pending = carry
                after = column_modes(ext, 3 * half, x, y + 1)
                forces = apply_modes(element_modes(before, after))
                scale = ext[6, x, y]
                later = []
                for c in range(3):
                    parts = []
                    for mx in (0, 1):
                        done = []
                        for mz in (0, 1):
                            odd = forces[c, mx, 1, mz] * scale
                            if (c, mx, 0, mz) in forces:
                                even = forces[c, mx, 0, mz] * scale
                                low, high = even - odd, even + odd
                            else:
                                low, high = -odd, odd
                            done.append(low + pending[c * 4 + mx * 2 + mz])
                            later.append(high)
                        parts.append((done[0] - done[1]) + from_below(done[0] + done[1]))
                    index = 3 * half + c
                    image[index, x, y] = carry_x[index, y] + (parts[0] - parts[1])
                    carry_x[index, y] = parts[0] + parts[1]
                return after, tuple(later)

            lax.fori_loop(
                0, size_y + 1, body, (column_modes(ext, 3 * half, x, 0), (zero,) * 12)
            )

    def node(column, totals):
        x, y = column // size_y, column % size_y
        around = (ext[6, x, y] + ext[6, x, y + 1]) + (ext[6, x + 1, y] + ext[6, x + 1, y + 1])
        inverse = 1.0 / ((around + from_below(around)) * DIAGONAL)
        norm, curve, cross, square = totals
        for c in range(3):
            residual = load[column, pl.ds(c * rows, rows), :] - image[c, x + 1, y + 1]
            stiff = image[3 + c, x + 1, y + 1]
            scaled, other = residual * inverse, stiff * inverse
            pair[c, x, y] = scaled
            pair[3 + c, x, y] = other
            norm = norm + residual * scaled
            curve = curve + ext[3 + c, x + 1, y + 1] * stiff
            cross = cross + residual * other
            square = square + stiff * other
        return norm, curve, cross, square

    totals = lax.fori_loop(0, size_x * size_y, node, (zero,) * 4)

    def pair_edge(delta, size):
        return (pl.ds(0, size), pl.ds(0, size)) if delta == 0 else (pl.ds(0, 1), pl.ds(size, 1))

    def pair_copy(number):
        dx, dy = LOWER[number]
        source_x, target_x = pair_edge(dx, size_x)
        source_y, target_y = pair_edge(dy, size_y)
        return pltpu.make_async_remote_copy(
            src_ref=pair.at[:, source_x, source_y],
            dst_ref=pair.at[:, target_x, target_y],
            send_sem=pair_send.at[number],
            recv_sem=pair_recv.at[number],
            device_id=(slab + dx, brick + dy),
            device_id_type=MESH,
        )

    for number, (dx, dy) in enumerate(LOWER):

        @pl.when(present(dx, dy))
        def _():
            pair_copy(number).start()

    for number, (dx, dy) in enumerate(LOWER):
        target_x, target_y = pair_edge(dx, size_x)[1], pair_edge(dy, size_y)[1]

        @pl.when(jnp.logical_not(present(-dx, -dy)))
        def _():
            shape = (6, target_x.size, target_y.size, rows, LANES)
            pair[:, target_x, target_y] = jnp.zeros(shape, jnp.float32)

    second_sums = sampled(pair, 0)

    for number, (dx, dy) in enumerate(LOWER):

        @pl.when(present(-dx, -dy))
        def _():
            pair_copy(number).wait_recv()

    def energy_row(x, energies):
        def body(y, carry):
            before, before_other, (first, mixed, last) = carry
            after = column_modes(pair, 0, x, y + 1)
            after_other = column_modes(pair, 3, x, y + 1)
            modes = element_modes(before, after)
            other = element_modes(before_other, after_other)
            scale = ext[6, x + 1, y + 1]
            forces, other_forces = apply_modes(modes), apply_modes(other)

            def dotted(left, right):
                total = None
                for key in TERMS:
                    term = left[key] * right[key]
                    total = term if total is None else total + term
                return total * scale

            first = first + dotted(modes, forces)
            mixed = mixed + dotted(other, forces)
            last = last + dotted(other, other_forces)
            return after, after_other, (first, mixed, last)

        start = (column_modes(pair, 0, x, 0), column_modes(pair, 3, x, 0), energies)
        return lax.fori_loop(0, size_y, body, start)[2]

    energies = lax.fori_loop(0, size_x, energy_row, (zero,) * 3)

    payload = jnp.concatenate([first_sums, second_sums], axis=0)
    for number, total in enumerate(totals + energies):
        payload = jnp.where(lane == 64 + number, jnp.sum(total, axis=1, keepdims=True), payload)

    def summed(value, part, me, count, send, recv, device):
        part[me] = value
        for step in range(1, count):
            pltpu.make_async_remote_copy(
                src_ref=part.at[me],
                dst_ref=part.at[me],
                send_sem=send.at[step - 1],
                recv_sem=recv.at[step - 1],
                device_id=device(lax.rem(me + step, count)),
                device_id_type=MESH,
            ).start()
        for step in range(1, count):
            source = lax.rem(me - step + count, count)
            pltpu.make_async_remote_copy(
                src_ref=part.at[source],
                dst_ref=part.at[source],
                send_sem=send.at[step - 1],
                recv_sem=recv.at[step - 1],
                device_id=device(source),
                device_id_type=MESH,
            ).wait_recv()
        total = part[0]
        for index in range(1, count):
            total = total + part[index]
        return total

    total = summed(payload, slab_part, slab, slabs, slab_send, slab_recv, lambda i: (i, brick))
    total = summed(total, brick_part, brick, bricks, brick_send, brick_recv, lambda i: (slab, i))

    frame_one = iota((rows, LANES), 0) >= tiles

    def scalar(number):
        column = total[:, 64 + number : 65 + number]
        return (
            jnp.sum(column[:tiles], axis=0, keepdims=True),
            jnp.sum(column[tiles:], axis=0, keepdims=True),
        )

    sums = [scalar(number) for number in range(7)]
    factors = []
    for frame in range(FRAMES):
        norm, curve, cross, square, first, mixed, last = [pairs[frame] for pairs in sums]
        step = norm / curve
        norm_next = norm - 2.0 * step * cross + step * step * square
        ratio = norm_next / norm
        curve_next = (
            (first - 2.0 * step * mixed + step * step * last)
            + 2.0 * ratio * (cross - step * square)
            + ratio * ratio * curve
        )
        step_next = norm_next / curve_next
        factors.append((step + step_next * ratio, step_next, -step_next * step))
    wide = [jnp.where(frame_one, factors[1][i], factors[0][i]) for i in range(3)]

    for frame in range(FRAMES):
        line = total[frame : frame + 1]
        for i in range(3):
            at = 2 * (i + 1) + frame
            line = line + factors[frame][i] * total[at : at + 1]
        sens_ref[frame : frame + 1, :] = line[:, :MUSCLES]

    flat_image = image.reshape(6 * (size_x + 1) * (size_y + 1) * rows, LANES)

    @pl.loop(0, size_x * size_y)
    def _(column):
        x, y = column // size_y, column % size_y
        for c in range(3):
            image[c, x, y] = (
                ext[c, x + 1, y + 1]
                + wide[0] * ext[3 + c, x + 1, y + 1]
                + wide[1] * pair[c, x, y]
                + wide[2] * pair[3 + c, x, y]
            )

    for frame in range(FRAMES):
        for c in range(3):
            for x in range(size_x):
                for tile in range(tiles):
                    base = (c * (size_x + 1) + x) * (size_y + 1) * rows + frame * tiles + tile
                    out_ref[frame, c, x, :, tile * LANES : (tile + 1) * LANES] = flat_image[
                        pl.ds(base, size_y, stride=rows), :
                    ]

    for number, (dx, dy) in enumerate(DIRECTIONS):

        @pl.when(present(dx, dy))
        def _():
            halo(number).wait_send()

    for number, (dx, dy) in enumerate(LOWER):

        @pl.when(present(dx, dy))
        def _():
            pair_copy(number).wait_send()

    for part, me, count, send, recv, device in (
        (slab_part, slab, slabs, slab_send, slab_recv, lambda i: (i, brick)),
        (brick_part, brick, bricks, brick_send, brick_recv, lambda i: (slab, i)),
    ):
        for step in range(1, count):
            pltpu.make_async_remote_copy(
                src_ref=part.at[me],
                dst_ref=part.at[me],
                send_sem=send.at[step - 1],
                recv_sem=recv.at[step - 1],
                device_id=device(lax.rem(me + step, count)),
                device_id_type=MESH,
            ).wait_send()


def on_device(slabs, bricks, occupancy, modulus, start, direction, force, line, attachments):
    size_x, size_y, size_z = occupancy.shape
    tiles = size_z // LANES
    rows = FRAMES * tiles
    vmem = pl.BlockSpec(memory_space=pltpu.VMEM)
    dma = pltpu.SemaphoreType.DMA
    return pl.pallas_call(
        functools.partial(kernel, slabs, bricks),
        out_shape=(
            jax.ShapeDtypeStruct(start.shape, jnp.float32),
            jax.ShapeDtypeStruct(force.shape, jnp.float32),
        ),
        in_specs=[vmem] * 7,
        out_specs=(vmem, vmem),
        scratch_shapes=[
            pltpu.VMEM((7, size_x + 2, size_y + 2, rows, LANES), jnp.float32),
            pltpu.VMEM((6, size_x + 1, size_y + 1, rows, LANES), jnp.float32),
            pltpu.VMEM((6, size_y + 1, rows, LANES), jnp.float32),
            pltpu.VMEM((6, size_x + 1, size_y + 1, rows, LANES), jnp.float32),
            pltpu.VMEM((size_x * size_y, 3 * rows, LANES), jnp.float32),
            pltpu.VMEM((size_x * size_y, MUSCLES * tiles, LANES), jnp.float32),
            pltpu.VMEM((slabs, rows, LANES), jnp.float32),
            pltpu.VMEM((bricks, rows, LANES), jnp.float32),
            dma((8,)),
            dma((8,)),
            dma((3,)),
            dma((3,)),
            dma((slabs - 1,)),
            dma((slabs - 1,)),
            dma((bricks - 1,)),
            dma((bricks - 1,)),
        ],
        compiler_params=pltpu.CompilerParams(
            collective_id=0, has_side_effects=True, vmem_limit_bytes=40 * 1024 * 1024
        ),
    )(
        occupancy,
        modulus,
        start,
        direction,
        force,
        jnp.transpose(line, (2, 0, 1)).reshape(3 * FRAMES, MUSCLES),
        jnp.transpose(attachments, (2, 0, 1)),
    )


def solution(mesh):
    return jax.shard_map(
        functools.partial(on_device, mesh.shape["slab"], mesh.shape["brick"]),
        mesh=mesh,
        in_specs=(
            P("slab", "brick", None),
            P("slab", "brick", None),
            P(None, None, "slab", "brick", None),
            P(None, None, "slab", "brick", None),
            P(),
            P(),
            P(),
        ),
        out_specs=(P(None, None, "slab", "brick", None), P()),
        check_vma=False,
    )
```

time: 325 us -> 66 us (0.20); the launches traced: 318 us -> 65.7 us
  blocking collectives: 164 us -> 0 us
  Pallas kernels: 0 us -> 57.9 us
  starting transfers between devices: 42.2 us -> 0 us
  local copies, waits for them, and re-layouts: 49 us -> 7.16 us
  matrix products: 27.2 us -> 0 us
  other arithmetic: 18.8 us -> 0 us
  waiting for transfers between devices: 14.7 us -> 0 us
    psum x4 -> x0, blocking collectives: 164 us -> none  [the longest x2 82 us: norm_total(): return lax.psum(frame_sums(residual, preconditioned), ('slab', 'brick'))]
    pallas_call x0 -> x1, Pallas kernels: none -> 57.9 us  [on_device(): pl.pallas_call(functools.partial(kernel, slabs, bricks), out_shape=(jax.S...]
    ppermute x14 -> x0, starting transfers between devices: 42.2 us -> none  [passed_along(): lax.ppermute(value, axis, [(source, source + steps) for source in range(l...]
    another operation x21 -> x0, local copies, waits for them, and re-layouts: 35.9 us -> none  [element_forces(): jnp.stack([extended[:, :, step_x:step_x + extent_x, step_y:step_y + exten...]
    dot_general x5 -> x0, matrix products: 27.2 us -> none  [the longest x3 15.2 us: element_forces(): jnp.einsum('biaj,afjxyz->bfixyz', blocked_stiffness, stacked, precision=l...]
    ppermute x14 -> x0, waiting for transfers between devices: 14.7 us -> none  [passed_along(): lax.ppermute(value, axis, [(source, source + steps) for source in range(l...]
    mul x3 -> x0, other arithmetic: 7.77 us -> none  [the longest x2 6.19 us: element_forces(): forces = forces * element_scale[None, None, None]]
    add x10 -> x0, other arithmetic: 7.17 us -> none  [the longest x3 3.48 us: element_forces(): summed = padded if summed is None else summed + padded]
  transfers between devices with their start and end apart: 14 -> 0, of which waited for: 7 -> 0; matrix products, arithmetic and copies ran while one was open for 8% -> 0% of each run, Pallas kernels for 0% -> 0%
where the time goes in v1:
time: 66 us; the launch traced here: 65.7 us
  Pallas kernels  57.9 us (88%)
  local copies, waits for them, and re-layouts  7.16 us (11%)
    pallas_call x1, Pallas kernels, on_device(): pl.pallas_call(functools.partial(kernel, slabs, bricks), out_shape=(jax.S...  57.9 us
    unnamed x16, local copies, waits for them, and re-layouts  7.15 us

profile of v1, /device:TPU:0, one launch (start us, length us, event | category | flops | bytes accessed | tf_op | source)
XLA Modules:
  0.0 65.7 jit_solution(10843804107843775139)
XLA Ops:
  0.6 0.0 copy-start.6
  0.6 0.7 %copy-done.6 = f32[2,40,3]{1,0,2:T(2,128)S(1)} copy-done((f32[2,40,3]{1,0,2:T(2,128)S(1)}, f32[2,40,3]{1,0,2:T(2,128)}, u32[]{:S(2)}) %copy-start.6) | copy-done | bytes 984
  1.3 0.0 copy-start.5
  1.3 0.7 %copy-done.5 = f32[2,40]{1,0:T(2,128)S(1)} copy-done((f32[2,40]{1,0:T(2,128)S(1)}, f32[2,40]{1,0:T(2,128)}, u32[]{:S(2)}) %copy-start.5) | copy-done | bytes 344
  2.0 0.0 copy-start
  2.0 1.0 %copy-done = f32[2,3,4,8,512]{4,3,2,1,0:T(8,128)S(1)} copy-done((f32[2,3,4,8,512]{4,3,2,1,0:T(8,128)S(1)}, f32[2,3,4,8,512]{4,3,2,1,0:T(8,128)}, u32[]{:S(2)}) %copy-start) | copy-done | bytes 393240
  3.0 0.0 copy-start.1
  3.0 1.0 %copy-done.1 = f32[2,3,4,8,512]{4,3,2,1,0:T(8,128)S(1)} copy-done((f32[2,3,4,8,512]{4,3,2,1,0:T(8,128)S(1)}, f32[2,3,4,8,512]{4,3,2,1,0:T(8,128)}, u32[]{:S(2)}) %copy-start.1) | copy-done | bytes 393240
  4.0 0.0 copy-start.2
  4.0 0.8 %copy-done.2 = s32[4,8,512]{2,1,0:T(8,128)S(1)} copy-done((s32[4,8,512]{2,1,0:T(8,128)S(1)}, s32[4,8,512]{2,1,0:T(8,128)}, u32[]{:S(2)}) %copy-start.2) | copy-done | bytes 65560
  4.8 0.0 copy-start.3
  4.8 0.8 %copy-done.3 = f32[4,8,512]{2,1,0:T(8,128)S(1)} copy-done((f32[4,8,512]{2,1,0:T(8,128)S(1)}, f32[4,8,512]{2,1,0:T(8,128)}, u32[]{:S(2)}) %copy-start.3) | copy-done | bytes 65560
  5.7 0.0 copy-start.4
  5.7 0.8 %copy-done.4 = s32[40,128,3]{1,0,2:T(8,128)S(1)} copy-done((s32[40,128,3]{1,0,2:T(8,128)S(1)}, s32[40,128,3]{1,0,2:T(8,128)}, u32[]{:S(2)}) %copy-start.4) | copy-done | bytes 61464
  6.5 57.9 %shard_map.86 = (f32[2,3,4,8,512]{4,3,2,1,0:T(8,128)S(1)}, f32[2,40]{1,0:T(2,128)S(1)}) custom-call(s32[4,8,512]{2,1,0:T(8,128)S(1)} %copy-done.2, f32[4,8,512]{2,1,0:T(8,128)S(1)} %copy-done.3, f32[2,3,4,8,512]{4,3,2,1,0:T(8,128)S(1)} %copy-done, f32[2,3,4,8,512]{4,3,2,1,0:T(8,128)S(1)} %copy-done.1, f32[2,40]{1,0:T(2,128)S(1)} %copy-done.5, ...), custom_call_target="tpu_custom_call" | custom-call | tf_op jit(solution)/shard_map/pallas_call | solution.py:586
  64.4 0.7 %copy.11 = f32[2,3,4,8,512]{4,3,2,1,0:T(8,128)} copy(f32[2,3,4,8,512]{4,3,2,1,0:T(8,128)S(1)} %get-tuple-element.4) | data formatting | bytes 786432
  65.1 0.6 copy.12
  (1 shorter events, 0.0 us)
Async XLA Ops:
  0.6 0.7 %copy-start.6 = (f32[2,40,3]{1,0,2:T(2,128)S(1)}, f32[2,40,3]{1,0,2:T(2,128)}, u32[]{:S(2)}) copy-start(f32[2,40,3]{1,0,2:T(2,128)} %param.12) | copy-start | bytes 2884
  1.3 0.7 %copy-start.5 = (f32[2,40]{1,0:T(2,128)S(1)}, f32[2,40]{1,0:T(2,128)}, u32[]{:S(2)}) copy-start(f32[2,40]{1,0:T(2,128)} %force_ref.1) | copy-start | bytes 964
  2.0 1.0 %copy-start = (f32[2,3,4,8,512]{4,3,2,1,0:T(8,128)S(1)}, f32[2,3,4,8,512]{4,3,2,1,0:T(8,128)}, u32[]{:S(2)}) copy-start(f32[2,3,4,8,512]{4,3,2,1,0:T(8,128)} %start_ref.1) | copy-start | bytes 1179652
  3.0 1.0 %copy-start.1 = (f32[2,3,4,8,512]{4,3,2,1,0:T(8,128)S(1)}, f32[2,3,4,8,512]{4,3,2,1,0:T(8,128)}, u32[]{:S(2)}) copy-start(f32[2,3,4,8,512]{4,3,2,1,0:T(8,128)} %dir_ref.1) | copy-start | bytes 1179652
  4.0 0.8 %copy-start.2 = (s32[4,8,512]{2,1,0:T(8,128)S(1)}, s32[4,8,512]{2,1,0:T(8,128)}, u32[]{:S(2)}) copy-start(s32[4,8,512]{2,1,0:T(8,128)} %occ_ref.1) | copy-start | bytes 196612
  4.8 0.8 %copy-start.3 = (f32[4,8,512]{2,1,0:T(8,128)S(1)}, f32[4,8,512]{2,1,0:T(8,128)}, u32[]{:S(2)}) copy-start(f32[4,8,512]{2,1,0:T(8,128)} %mod_ref.1) | copy-start | bytes 196612
  5.7 0.8 %copy-start.4 = (s32[40,128,3]{1,0,2:T(8,128)S(1)}, s32[40,128,3]{1,0,2:T(8,128)}, u32[]{:S(2)}) copy-start(s32[40,128,3]{1,0,2:T(8,128)} %param.13) | copy-start | bytes 184324

commit v2 on v1

--- a/solution.py
+++ b/solution.py
@@ -13,6 +13,8 @@
 ATTACH = 128
 FRAMES = 2
 LANES = 128
+UNROLL_IMAGE = 3
+UNROLL_ENERGY = 4
 
 ersatz_modulus = 0.02
 MESH = pl.DeviceIdType.MESH
@@ -112,15 +114,23 @@
 def kernel(
     slabs,
     bricks,
+    start_in,
+    dir_in,
+    occ_in,
+    mod_in,
+    att_in,
+    force_in,
+    line_in,
+    out_ref,
+    sens_ref,
+    start_ref,
+    dir_ref,
     occ_ref,
     mod_ref,
-    start_ref,
-    dir_ref,
+    att_ref,
     force_ref,
     line_ref,
-    att_ref,
-    out_ref,
-    sens_ref,
+    fetched,
     ext,
     image,
     carry_x,
@@ -144,6 +154,14 @@
     slab = lax.axis_index("slab")
     brick = lax.axis_index("brick")
     barrier = pltpu.get_barrier_semaphore()
+    sources = (start_in, dir_in, occ_in, mod_in, att_in, force_in, line_in)
+    targets = (start_ref, dir_ref, occ_ref, mod_ref, att_ref, force_ref, line_ref)
+    fetches = [
+        pltpu.make_async_copy(source, target, fetched.at[number])
+        for number, (source, target) in enumerate(zip(sources, targets))
+    ]
+    for fetch in fetches:
+        fetch.start()
 
     def present(dx, dy):
         ok = None
@@ -177,6 +195,9 @@
     def place(field, x, row, value):
         base = ((field * (size_x + 2) + x + 1) * (size_y + 2) + 1) * rows + row
         flat[pl.ds(base, size_y, stride=rows), :] = value
+
+    for fetch in fetches[:4]:
+        fetch.wait()
 
     for x in range(size_x):
         for tile in range(tiles):
@@ -235,7 +256,10 @@
     lane_ids = lax.broadcasted_iota(jnp.int32, (LANES, width), 0)
     second = (lax.broadcasted_iota(jnp.int32, (1, width), 1) >= ATTACH).astype(jnp.int32)
 
-    @pl.loop(0, MUSCLES // 2)
+    for fetch in fetches[4:]:
+        fetch.wait()
+
+    @pl.loop(0, MUSCLES // 2, unroll=4)
     def _(two):
         def both(dim):
             return jnp.concatenate(
@@ -270,12 +294,12 @@
     spread_rows = ones_where(iota((24, 6), 0) // tiles == iota((24, 6), 1))
     spread_cols = ones_where(iota((MUSCLES, span), 1) // tiles == iota((MUSCLES, span), 0))
     same_tile = ones_where(iota((24, span), 0) % tiles == iota((24, span), 1) % tiles)
-    lines = line_ref[...] * (1.0 / ATTACH)
+    lines = jnp.concatenate([line_ref[c] for c in range(3)], axis=0) * (1.0 / ATTACH)
     forces = jnp.concatenate([force_ref[...]] * 3, axis=0)
     line_wide = dot32(spread_rows, dot32(lines, spread_cols)) * same_tile
     load_wide = split_rows(dot32(spread_rows, dot32(lines * forces, spread_cols)) * same_tile)
 
-    @pl.loop(0, size_x * size_y)
+    @pl.loop(0, size_x * size_y, unroll=8)
     def _(column):
         both = jnp.dot(
             load_wide, counts[column].astype(jnp.bfloat16), preferred_element_type=jnp.float32
@@ -294,7 +318,7 @@
             )
 
         both = lax.fori_loop(
-            0, size_x * size_y, body, jnp.zeros((12 * rows, span), jnp.float32)
+            0, size_x * size_y, body, jnp.zeros((12 * rows, span), jnp.float32), unroll=8
         )
         total = (both[: 6 * rows] + both[6 * rows :]) * jnp.concatenate([line_wide] * 2, axis=0)
         shape = (4, 6 * rows)
@@ -348,13 +372,13 @@
 
     @pl.loop(0, size_x + 1)
     def _(x):
-        for half in (0, 1):
-
-            def body(y, carry):
-                before, pending = carry
+        def body(y, carry):
+            after_both, later_both = [], []
+            scale = ext[6, x, y]
+            for half in (0, 1):
+                before, pending = carry[0][half], carry[1][half]
                 after = column_modes(ext, 3 * half, x, y + 1)
                 forces = apply_modes(element_modes(before, after))
-                scale = ext[6, x, y]
                 later = []
                 for c in range(3):
                     parts = []
@@ -373,11 +397,12 @@
                     index = 3 * half + c
                     image[index, x, y] = carry_x[index, y] + (parts[0] - parts[1])
                     carry_x[index, y] = parts[0] + parts[1]
-                return after, tuple(later)
-
-            lax.fori_loop(
-                0, size_y + 1, body, (column_modes(ext, 3 * half, x, 0), (zero,) * 12)
-            )
+                after_both.append(after)
+                later_both.append(tuple(later))
+            return tuple(after_both), tuple(later_both)
+
+        first = tuple(column_modes(ext, 3 * half, x, 0) for half in (0, 1))
+        lax.fori_loop(0, size_y + 1, body, (first, ((zero,) * 12,) * 2), unroll=UNROLL_IMAGE)
 
     def node(column, totals):
         x, y = column // size_y, column % size_y
@@ -396,7 +421,7 @@
             square = square + stiff * other
         return norm, curve, cross, square
 
-    totals = lax.fori_loop(0, size_x * size_y, node, (zero,) * 4)
+    totals = lax.fori_loop(0, size_x * size_y, node, (zero,) * 4, unroll=4)
 
     def pair_edge(delta, size):
         return (pl.ds(0, size), pl.ds(0, size)) if delta == 0 else (pl.ds(0, 1), pl.ds(size, 1))
@@ -459,7 +484,7 @@
             return after, after_other, (first, mixed, last)
 
         start = (column_modes(pair, 0, x, 0), column_modes(pair, 3, x, 0), energies)
-        return lax.fori_loop(0, size_y, body, start)[2]
+        return lax.fori_loop(0, size_y, body, start, unroll=UNROLL_ENERGY)[2]
 
     energies = lax.fori_loop(0, size_x, energy_row, (zero,) * 3)
 
@@ -530,7 +555,7 @@
 
     flat_image = image.reshape(6 * (size_x + 1) * (size_y + 1) * rows, LANES)
 
-    @pl.loop(0, size_x * size_y)
+    @pl.loop(0, size_x * size_y, unroll=4)
     def _(column):
         x, y = column // size_y, column % size_y
         for c in range(3):
@@ -589,9 +614,17 @@
             jax.ShapeDtypeStruct(start.shape, jnp.float32),
             jax.ShapeDtypeStruct(force.shape, jnp.float32),
         ),
-        in_specs=[vmem] * 7,
+        in_specs=[pl.BlockSpec(memory_space=pltpu.HBM)] * 7,
         out_specs=(vmem, vmem),
         scratch_shapes=[
+            pltpu.VMEM(start.shape, jnp.float32),
+            pltpu.VMEM(start.shape, jnp.float32),
+            pltpu.VMEM(occupancy.shape, jnp.int32),
+            pltpu.VMEM(occupancy.shape, jnp.float32),
+            pltpu.VMEM((3, MUSCLES, ATTACH), jnp.int32),
+            pltpu.VMEM((FRAMES, MUSCLES), jnp.float32),
+            pltpu.VMEM((3, FRAMES, MUSCLES), jnp.float32),
+            dma((7,)),
             pltpu.VMEM((7, size_x + 2, size_y + 2, rows, LANES), jnp.float32),
             pltpu.VMEM((6, size_x + 1, size_y + 1, rows, LANES), jnp.float32),
             pltpu.VMEM((6, size_y + 1, rows, LANES), jnp.float32),
@@ -610,16 +643,16 @@
             dma((bricks - 1,)),
         ],
         compiler_params=pltpu.CompilerParams(
-            collective_id=0, has_side_effects=True, vmem_limit_bytes=40 * 1024 * 1024
+            collective_id=0, has_side_effects=True, vmem_limit_bytes=60 * 1024 * 1024
         ),
     )(
+        start,
+        direction,
         occupancy,
         modulus,
-        start,
-        direction,
+        jnp.transpose(attachments, (2, 0, 1)),
         force,
-        jnp.transpose(line, (2, 0, 1)).reshape(3 * FRAMES, MUSCLES),
-        jnp.transpose(attachments, (2, 0, 1)),
+        jnp.transpose(line, (2, 0, 1)),
     )
 
 

time: 66 us -> 45.2 us (0.68)
  Pallas kernels: 57.9 us -> 42.1 us
  local copies, waits for them, and re-layouts: 7.16 us -> 2.34 us
    pallas_call x1, Pallas kernels: 57.9 us -> 42.1 us  [on_device(): pl.pallas_call(functools.partial(kernel, slabs, bricks), out_shape=(jax.S...]
    unnamed x16 -> x4, local copies, waits for them, and re-layouts: 7.15 us -> 2.34 us
where the time goes in v2:
time: 45.2 us; the launch traced here: 45.1 us
  Pallas kernels  42.1 us (93%)
  local copies, waits for them, and re-layouts  2.34 us (5%)
  between operations  0.65 us (1%)
    pallas_call x1, Pallas kernels, on_device(): pl.pallas_call(functools.partial(kernel, slabs, bricks), out_shape=(jax.S...  42.1 us
    unnamed x4, local copies, waits for them, and re-layouts  2.34 us

profile of v2, /device:TPU:0, one launch (start us, length us, event | category | flops | bytes accessed | tf_op | source)
XLA Modules:
  0.0 45.1 jit_solution(18335369194150223048)
XLA Ops:
  0.6 42.1 %shard_map.86 = (f32[2,3,4,8,512]{4,3,2,1,0:T(8,128)}, f32[2,40]{1,0:T(2,128)}) custom-call(f32[2,3,4,8,512]{4,3,2,1,0:T(8,128)} %start_in.1, f32[2,3,4,8,512]{4,3,2,1,0:T(8,128)} %dir_in.1, s32[4,8,512]{2,1,0:T(8,128)} %occ_in.1, f32[4,8,512]{2,1,0:T(8,128)} %mod_in.1, s32[3,40,128]{2,1,0:T(8,128)} %bitcast.2, f32[2,40]{1,0:T(2,128)} %force_in.1, ...), custom_call_target="tpu_custom_call" | custom-call | tf_op jit(solution)/shard_map/pallas_call | solution.py:611
  42.7 0.0 copy-start
  42.7 1.8 %copy.11 = f32[2,3,4,8,512]{4,3,2,1,0:T(8,128)} copy(f32[2,3,4,8,512]{4,3,2,1,0:T(8,128)} %get-tuple-element.4) | data formatting | bytes 786432
  44.5 0.0 copy-done
  44.5 0.6 %copy.12 = f32[2,40]{1,0:T(2,128)} copy(f32[2,40]{1,0:T(2,128)S(1)} %copy-done) | data formatting | bytes 640
Async XLA Ops:
  42.7 1.8 %copy-start = (f32[2,40]{1,0:T(2,128)S(1)}, f32[2,40]{1,0:T(2,128)}, u32[]{:S(2)}) copy-start(f32[2,40]{1,0:T(2,128)} %get-tuple-element.5) | copy-start | bytes 964

commit v3 on v2

--- a/solution.py
+++ b/solution.py
@@ -362,16 +362,15 @@
                     modes[c, mx, 1, mz] = high - low
         return modes
 
-    for number, (dx, dy) in enumerate(DIRECTIONS):
-
-        @pl.when(present(-dx, -dy))
-        def _():
-            halo(number).wait_recv()
-
-    carry_x[...] = jnp.zeros_like(carry_x)
-
-    @pl.loop(0, size_x + 1)
-    def _(x):
+    def wait_halos(wanted):
+        for number, (dx, dy) in enumerate(DIRECTIONS):
+            if dx in wanted:
+
+                @pl.when(present(-dx, -dy))
+                def _():
+                    halo(number).wait_recv()
+
+    def image_row(x, lowest=False):
         def body(y, carry):
             after_both, later_both = [], []
             scale = ext[6, x, y]
@@ -395,8 +394,11 @@
                             later.append(high)
                         parts.append((done[0] - done[1]) + from_below(done[0] + done[1]))
                     index = 3 * half + c
-                    image[index, x, y] = carry_x[index, y] + (parts[0] - parts[1])
-                    carry_x[index, y] = parts[0] + parts[1]
+                    if lowest:
+                        image[index, 1, y] += parts[0] + parts[1]
+                    else:
+                        image[index, x, y] = carry_x[index, y] + (parts[0] - parts[1])
+                        carry_x[index, y] = parts[0] + parts[1]
                 after_both.append(after)
                 later_both.append(tuple(later))
             return tuple(after_both), tuple(later_both)
@@ -421,8 +423,6 @@
             square = square + stiff * other
         return norm, curve, cross, square
 
-    totals = lax.fori_loop(0, size_x * size_y, node, (zero,) * 4, unroll=4)
-
     def pair_edge(delta, size):
         return (pl.ds(0, size), pl.ds(0, size)) if delta == 0 else (pl.ds(0, 1), pl.ds(size, 1))
 
@@ -439,11 +439,32 @@
             device_id_type=MESH,
         )
 
-    for number, (dx, dy) in enumerate(LOWER):
-
-        @pl.when(present(dx, dy))
-        def _():
-            pair_copy(number).start()
+    def start_pair(numbers):
+        for number in numbers:
+
+            @pl.when(present(*LOWER[number]))
+            def _():
+                pair_copy(number).start()
+
+    def wait_pair(numbers):
+        for number in numbers:
+            dx, dy = LOWER[number]
+
+            @pl.when(present(-dx, -dy))
+            def _():
+                pair_copy(number).wait_recv()
+
+    carry_x[...] = jnp.zeros_like(carry_x)
+    wait_halos((0,))
+    pl.loop(1, size_x)(image_row)
+    wait_halos((1,))
+    image_row(0, lowest=True)
+    totals = lax.fori_loop(0, size_y, node, (zero,) * 4, unroll=4)
+    start_pair((0, 2))
+    wait_halos((-1,))
+    image_row(size_x)
+    totals = lax.fori_loop(size_y, size_x * size_y, node, totals, unroll=4)
+    start_pair((1,))
 
     for number, (dx, dy) in enumerate(LOWER):
         target_x, target_y = pair_edge(dx, size_x)[1], pair_edge(dy, size_y)[1]
@@ -454,12 +475,6 @@
             pair[:, target_x, target_y] = jnp.zeros(shape, jnp.float32)
 
     second_sums = sampled(pair, 0)
-
-    for number, (dx, dy) in enumerate(LOWER):
-
-        @pl.when(present(-dx, -dy))
-        def _():
-            pair_copy(number).wait_recv()
 
     def energy_row(x, energies):
         def body(y, carry):
@@ -486,7 +501,10 @@
         start = (column_modes(pair, 0, x, 0), column_modes(pair, 3, x, 0), energies)
         return lax.fori_loop(0, size_y, body, start, unroll=UNROLL_ENERGY)[2]
 
-    energies = lax.fori_loop(0, size_x, energy_row, (zero,) * 3)
+    wait_pair((1,))
+    energies = lax.fori_loop(0, size_x - 1, energy_row, (zero,) * 3)
+    wait_pair((0, 2))
+    energies = energy_row(size_x - 1, energies)
 
     payload = jnp.concatenate([first_sums, second_sums], axis=0)
     for number, total in enumerate(totals + energies):

time: 45.2 us -> 39 us (0.86)
  Pallas kernels: 42.1 us -> 35.9 us
    pallas_call x1, Pallas kernels: 42.1 us -> 35.9 us  [on_device(): pl.pallas_call(functools.partial(kernel, slabs, bricks), out_shape=(jax.S...]
where the time goes in v3:
time: 39 us; the launch traced here: 38.9 us
  Pallas kernels  35.9 us (92%)
  local copies, waits for them, and re-layouts  2.34 us (6%)
  between operations  0.65 us (2%)
    pallas_call x1, Pallas kernels, on_device(): pl.pallas_call(functools.partial(kernel, slabs, bricks), out_shape=(jax.S...  35.9 us
    unnamed x4, local copies, waits for them, and re-layouts  2.34 us

profile of v3, /device:TPU:0, one launch (start us, length us, event | category | flops | bytes accessed | tf_op | source)
XLA Modules:
  0.0 38.9 jit_solution(6599797881584561933)
XLA Ops:
  0.6 35.9 %shard_map.86 = (f32[2,3,4,8,512]{4,3,2,1,0:T(8,128)}, f32[2,40]{1,0:T(2,128)}) custom-call(f32[2,3,4,8,512]{4,3,2,1,0:T(8,128)} %start_in.1, f32[2,3,4,8,512]{4,3,2,1,0:T(8,128)} %dir_in.1, s32[4,8,512]{2,1,0:T(8,128)} %occ_in.1, f32[4,8,512]{2,1,0:T(8,128)} %mod_in.1, s32[3,40,128]{2,1,0:T(8,128)} %bitcast.2, f32[2,40]{1,0:T(2,128)} %force_in.1, ...), custom_call_target="tpu_custom_call" | custom-call | tf_op jit(solution)/shard_map/pallas_call | solution.py:629
  36.5 0.0 copy-start
  36.5 1.8 %copy.11 = f32[2,3,4,8,512]{4,3,2,1,0:T(8,128)} copy(f32[2,3,4,8,512]{4,3,2,1,0:T(8,128)} %get-tuple-element.4) | data formatting | bytes 786432
  38.3 0.0 copy-done
  38.3 0.6 %copy.12 = f32[2,40]{1,0:T(2,128)} copy(f32[2,40]{1,0:T(2,128)S(1)} %copy-done) | data formatting | bytes 640
Async XLA Ops:
  36.5 1.8 %copy-start = (f32[2,40]{1,0:T(2,128)S(1)}, f32[2,40]{1,0:T(2,128)}, u32[]{:S(2)}) copy-start(f32[2,40]{1,0:T(2,128)} %get-tuple-element.5) | copy-start | bytes 964

commit v4 on v3

--- a/solution.py
+++ b/solution.py
@@ -19,7 +19,7 @@
 ersatz_modulus = 0.02
 MESH = pl.DeviceIdType.MESH
 HIGHEST = lax.Precision.HIGHEST
-DIRECTIONS = [(dx, dy) for dx in (-1, 0, 1) for dy in (-1, 0, 1) if (dx, dy) != (0, 0)]
+DIRECTIONS = [(dx, dy) for dx in (0, 1, -1) for dy in (0, 1, -1) if (dx, dy) != (0, 0)]
 LOWER = [(-1, 0), (0, -1), (-1, -1)]
 
 
@@ -259,7 +259,7 @@
     for fetch in fetches[4:]:
         fetch.wait()
 
-    @pl.loop(0, MUSCLES // 2, unroll=4)
+    @pl.loop(0, MUSCLES // 2, unroll=10)
     def _(two):
         def both(dim):
             return jnp.concatenate(
@@ -299,7 +299,7 @@
     line_wide = dot32(spread_rows, dot32(lines, spread_cols)) * same_tile
     load_wide = split_rows(dot32(spread_rows, dot32(lines * forces, spread_cols)) * same_tile)
 
-    @pl.loop(0, size_x * size_y, unroll=8)
+    @pl.loop(0, size_x * size_y, unroll=16)
     def _(column):
         both = jnp.dot(
             load_wide, counts[column].astype(jnp.bfloat16), preferred_element_type=jnp.float32
@@ -318,7 +318,7 @@
             )
 
         both = lax.fori_loop(
-            0, size_x * size_y, body, jnp.zeros((12 * rows, span), jnp.float32), unroll=8
+            0, size_x * size_y, body, jnp.zeros((12 * rows, span), jnp.float32), unroll=16
         )
         total = (both[: 6 * rows] + both[6 * rows :]) * jnp.concatenate([line_wide] * 2, axis=0)
         shape = (4, 6 * rows)
@@ -459,11 +459,11 @@
     pl.loop(1, size_x)(image_row)
     wait_halos((1,))
     image_row(0, lowest=True)
-    totals = lax.fori_loop(0, size_y, node, (zero,) * 4, unroll=4)
+    totals = lax.fori_loop(0, size_y, node, (zero,) * 4, unroll=8)
     start_pair((0, 2))
     wait_halos((-1,))
     image_row(size_x)
-    totals = lax.fori_loop(size_y, size_x * size_y, node, totals, unroll=4)
+    totals = lax.fori_loop(size_y, size_x * size_y, node, totals, unroll=8)
     start_pair((1,))
 
     for number, (dx, dy) in enumerate(LOWER):
@@ -573,7 +573,7 @@
 
     flat_image = image.reshape(6 * (size_x + 1) * (size_y + 1) * rows, LANES)
 
-    @pl.loop(0, size_x * size_y, unroll=4)
+    @pl.loop(0, size_x * size_y, unroll=8)
     def _(column):
         x, y = column // size_y, column % size_y
         for c in range(3):

time: 39 us -> 36 us (0.923)
  Pallas kernels: 35.9 us -> 32.8 us
    pallas_call x1, Pallas kernels: 35.9 us -> 32.8 us  [on_device(): pl.pallas_call(functools.partial(kernel, slabs, bricks), out_shape=(jax.S...]
where the time goes in v4:
time: 36 us; the launch traced here: 35.8 us
  Pallas kernels  32.8 us (91%)
  local copies, waits for them, and re-layouts  2.34 us (6%)
  between operations  0.65 us (2%)
    pallas_call x1, Pallas kernels, on_device(): pl.pallas_call(functools.partial(kernel, slabs, bricks), out_shape=(jax.S...  32.8 us
    unnamed x4, local copies, waits for them, and re-layouts  2.34 us

profile of v4, /device:TPU:0, one launch (start us, length us, event | category | flops | bytes accessed | tf_op | source)
XLA Modules:
  0.0 35.8 jit_solution(9144254083526230145)
XLA Ops:
  0.6 32.8 %shard_map.86 = (f32[2,3,4,8,512]{4,3,2,1,0:T(8,128)}, f32[2,40]{1,0:T(2,128)}) custom-call(f32[2,3,4,8,512]{4,3,2,1,0:T(8,128)} %start_in.1, f32[2,3,4,8,512]{4,3,2,1,0:T(8,128)} %dir_in.1, s32[4,8,512]{2,1,0:T(8,128)} %occ_in.1, f32[4,8,512]{2,1,0:T(8,128)} %mod_in.1, s32[3,40,128]{2,1,0:T(8,128)} %bitcast.2, f32[2,40]{1,0:T(2,128)} %force_in.1, ...), custom_call_target="tpu_custom_call" | custom-call | tf_op jit(solution)/shard_map/pallas_call | solution.py:629
  33.5 0.0 copy-start
  33.5 1.8 %copy.11 = f32[2,3,4,8,512]{4,3,2,1,0:T(8,128)} copy(f32[2,3,4,8,512]{4,3,2,1,0:T(8,128)} %get-tuple-element.4) | data formatting | bytes 786432
  35.3 0.0 copy-done
  35.3 0.6 %copy.12 = f32[2,40]{1,0:T(2,128)} copy(f32[2,40]{1,0:T(2,128)S(1)} %copy-done) | data formatting | bytes 640
Async XLA Ops:
  33.5 1.8 %copy-start = (f32[2,40]{1,0:T(2,128)S(1)}, f32[2,40]{1,0:T(2,128)}, u32[]{:S(2)}) copy-start(f32[2,40]{1,0:T(2,128)} %get-tuple-element.5) | copy-start | bytes 964
